TPU v7x, 32 devices: a whole 2x2x4 slice. The times are simulated.
32 devices in a mesh: seq: 8 (over z, y), head: 4 (over x, core).
Axes of the slice: x: 2, y: 2, z: 4, core: 2. Of those that a mesh axis runs over, the one named last changes fastest.
Arguments:
- queries: bfloat16 [1024, 1024], P('seq', 'head'), may hold values from -16 to 16
- key_vectors: bfloat16 [1024, 1024], P('seq', 'head'), may hold values from -16 to 16
- values: bfloat16 [1024, 1024], P('seq', 'head'), may hold values from -6 to 6
- step_rates: float32 [1024, 4], P('seq', 'head'), may hold values from 0.1 to 1
- fast_weights: float32 [4, 3, 256, 256], P('head', None, 'seq'), may hold values from -0.375 to 0.375
- momentum: float32 [4, 3, 256, 256], P('head', None, 'seq'), may hold values from -0.4375 to 0.4375
- momentum_decay: float32 [4], P('head'), may hold values from 0.5 to 0.95
- memory_gain: float32 [1024], P('head'), may hold values from 0.5 to 1.5
- window_gain: float32 [1024], P('head'), may hold values from 0.5 to 1.5
Outputs:
- blended: bfloat16 [1024, 1024], P('seq', 'head')
- new_weights: float32 [4, 3, 256, 256], P('head', None, 'seq')
- new_momentum: float32 [4, 3, 256, 256], P('head', None, 'seq')
All inputs are finite; a program needn't handle non-finite values.
Results may differ from a plain program's by a relative error of at most 0.0085.
Values may be sent and summed in bfloat16 or wider, within the bound.
A program may use at most 64 MiB of HBM per device.

v0:
```python
import math

import jax
import jax.numpy as jnp
from jax import lax
from jax.sharding import PartitionSpec as P

WINDOW = 512


def passed_along(value, axis, steps):
    count = lax.axis_size(axis)
    leading, last = (max(0, -steps), min(count, count - steps))
    return lax.ppermute(value, axis, [(source, source + steps) for source in range(leading, last)])


def silu_slope(field):
    sigmoid_x = jax.nn.sigmoid(field)
    return sigmoid_x * (1.0 + field * (1.0 - sigmoid_x))


def keep_scale(candidate, previous):
    old_rms = jnp.sqrt(jnp.mean(previous * previous, axis=-1, keepdims=True) + 1e-06)
    new_rms = jnp.sqrt(jnp.mean(candidate * candidate, axis=-1, keepdims=True) + 1e-06)
    return candidate * (old_rms / new_rms)


def rms_scale(field, gain):
    return field * lax.rsqrt(jnp.mean(field * field, axis=-1, keepdims=True) + 1e-06) * gain


def contract_rows(left, right):
    return lax.dot_general(
        left, right, (((0,), (0,)), ((), ())), preferred_element_type=jnp.float32
    )


def per_device(
    queries,
    key_vectors,
    values,
    step_rates,
    fast_weights,
    momentum,
    momentum_decay,
    memory_gain,
    window_gain,
):
    tokens_here, head_width = queries.shape
    seq_count = lax.axis_size("seq")
    my_index = lax.axis_index("seq")
    shard_rows = fast_weights.shape[2]
    inner_rate = 0.1 / math.sqrt(tokens_here * seq_count)
    hop_count = -(-WINDOW // tokens_here)
    border = (key_vectors, values)
    earlier = []
    for step_back in range(hop_count):
        earlier.append(passed_along((border[0], border[1]), "seq", step_back + 1))
    context_keys = jnp.concatenate(
        [piece[0] for piece in reversed(earlier)] + [key_vectors], axis=0
    )
    context_values = jnp.concatenate([piece[1] for piece in reversed(earlier)] + [values], axis=0)
    block_rows = min(tokens_here, max(WINDOW, 512))
    scores = lax.dot_general(
        queries, context_keys, (((1,), (1,)), ((), ())), preferred_element_type=jnp.float32
    ) * head_width ** (-0.5)
    query_pos = my_index * tokens_here + 0 + jnp.arange(block_rows, dtype=jnp.int32)
    key_pos = my_index * tokens_here + 0 - WINDOW + jnp.arange(block_rows + WINDOW, dtype=jnp.int32)
    distance = query_pos[:, None] - key_pos[None, :]
    allowed = (key_pos[None, :] >= 0) & (distance >= 0) & (distance < WINDOW)
    scores = jnp.where(allowed, scores, jnp.float32(-1e30))
    row_max = jnp.max(scores, axis=1, keepdims=True)
    weights = jnp.exp(scores - row_max)
    probabilities = (weights / jnp.sum(weights, axis=1, keepdims=True)).astype(jnp.bfloat16)
    attended_blocks = jnp.dot(probabilities, context_values, preferred_element_type=jnp.float32)
    owned = fast_weights[0]
    whole_weights, whole_moment = (
        lax.all_gather(owned, "seq", axis=1, tiled=True),
        lax.all_gather(momentum[0], "seq", axis=1, tiled=True),
    )
    gathered = whole_weights.astype(jnp.bfloat16)
    gate_pre = jnp.dot(key_vectors, gathered[0], preferred_element_type=jnp.float32)
    up_pre = jnp.dot(key_vectors, gathered[1], preferred_element_type=jnp.float32)
    gate_act = jax.nn.silu(gate_pre)
    hidden = (gate_act * up_pre).astype(jnp.bfloat16)
    target_grad = (-(inner_rate * step_rates) * values.astype(jnp.float32)).astype(jnp.bfloat16)
    hidden_grad = lax.dot_general(
        target_grad, gathered[2], (((1,), (1,)), ((), ())), preferred_element_type=jnp.float32
    )
    gate_grad = (hidden_grad * up_pre * silu_slope(gate_pre)).astype(jnp.bfloat16)
    up_grad = (hidden_grad * gate_act).astype(jnp.bfloat16)
    paired = jnp.concatenate([gate_grad, up_grad], axis=1)
    summed_all = lax.psum(
        jnp.concatenate(
            [contract_rows(key_vectors, paired), contract_rows(hidden, target_grad)], axis=1
        ),
        "seq",
    )
    gradient = summed_all.reshape(head_width, 3, head_width).transpose(1, 0, 2)
    moment_full = momentum_decay[0] * whole_moment + gradient
    weight_full = keep_scale(whole_weights - moment_full, whole_weights)
    updated = weight_full.astype(jnp.bfloat16)
    weight_new = lax.dynamic_slice_in_dim(weight_full, my_index * shard_rows, shard_rows, 1)
    moment_new = lax.dynamic_slice_in_dim(moment_full, my_index * shard_rows, shard_rows, 1)
    gate_out = jnp.dot(queries, updated[0], preferred_element_type=jnp.float32)
    up_out = jnp.dot(queries, updated[1], preferred_element_type=jnp.float32)
    inner_act = (jax.nn.silu(gate_out) * up_out).astype(jnp.bfloat16)
    recalled = jnp.dot(inner_act, updated[2], preferred_element_type=jnp.float32)
    blended = (rms_scale(recalled, memory_gain) + rms_scale(attended_blocks, window_gain)).astype(
        jnp.bfloat16
    )
    return (blended, weight_new[None], moment_new[None])


def solution(mesh):
    in_specs = (
        P("seq", "head"),
        P("seq", "head"),
        P("seq", "head"),
        P("seq", "head"),
        P("head", None, "seq", None),
        P("head", None, "seq", None),
        P("head"),
        P("head"),
        P("head"),
    )
    out_specs = (P("seq", "head"), P("head", None, "seq", None), P("head", None, "seq", None))
    return jax.shard_map(
        per_device, mesh=mesh, in_specs=in_specs, out_specs=out_specs, check_vma=False
    )
```

profile of v0, /device:TPU:0, one launch (start us, length us, event | category | flops | bytes accessed | tf_op | source)
XLA Modules:
  0.0 147.7 jit_solution(8238908626431817228)
XLA Ops:
  7.2 5.9 %collective-permute-start = (bf16[128,256]{1,0:T(8,128)(2,1)}, bf16[128,256]{1,0:T(8,128)(2,1)S(1)}, u32[]{:S(2)}, u32[]{:S(2)}) collective-permute-start(bf16[128,256]{1,0:T(8,128)(2,1)} %param.10), channel_id=1, source_target_pairs={{0,16},{4,20},{8,24},{12,28},{1,17},{5,21},{9,25},{13,29},{2,18},{... | collective-permute-start | bytes 196616 | tf_op jit(solution)/shard_map/ppermute | solution.py:14
  13.2 4.4 %collective-permute-start.1 = (bf16[128,256]{1,0:T(8,128)(2,1)}, bf16[128,256]{1,0:T(8,128)(2,1)S(1)}, u32[]{:S(2)}, u32[]{:S(2)}) collective-permute-start(bf16[128,256]{1,0:T(8,128)(2,1)} %param.10), channel_id=1, source_target_pairs={{0,12},{4,16},{8,20},{12,24},{16,28},{1,13},{5,17},{9,21},{13,25},... | collective-permute-start | bytes 196616 | tf_op jit(solution)/shard_map/ppermute | solution.py:14
  17.6 1.3 collective-permute-start.2
  18.9 3.1 %collective-permute-start.3 = (bf16[128,256]{1,0:T(8,128)(2,1)}, bf16[128,256]{1,0:T(8,128)(2,1)S(1)}, u32[]{:S(2)}, u32[]{:S(2)}) collective-permute-start(bf16[128,256]{1,0:T(8,128)(2,1)} %param.10), channel_id=1, source_target_pairs={{0,4},{4,8},{8,12},{12,16},{16,20},{20,24},{24,28},{1,5},{5,9},{9,... | collective-permute-start | bytes 196616 | tf_op jit(solution)/shard_map/ppermute | solution.py:14
  22.0 1.3 collective-permute-start.4
  23.3 32.4 %all-gather = f32[1,3,256,256]{3,2,1,0:T(8,128)S(1)} all-gather(f32[1,3,32,256]{3,2,1,0:T(8,128)} %param.13), channel_id=2, replica_groups=mesh['seq'=8,'head'=4] {'seq'}, dimensions={2}, use_global_device_ids=true | all-gather | bytes 884736 | tf_op jit(solution)/shard_map/all_gather | solution.py:78
  55.8 0.6 copy-done.6
  56.4 0.2 copy-done.1
  56.6 0.2 fusion.11
  56.8 0.7 copy-done.2
  57.4 0.2 fusion.12
  57.6 0.2 multiply_convert_fusion.2
  57.9 0.3 fusion.22
  58.2 0.3 convolution_bitcast_fusion
  58.5 1.2 copy.12
  59.7 0.8 copy-done.3
  60.5 33.4 %all-gather.1 = f32[1,3,256,256]{3,2,1,0:T(8,128)S(1)} all-gather(f32[1,3,32,256]{3,2,1,0:T(8,128)S(1)} %copy-done.3), channel_id=3, replica_groups=mesh['seq'=8,'head'=4] {'seq'}, dimensions={2}, use_global_device_ids=true | all-gather | bytes 884736 | tf_op jit(solution)/shard_map/all_gather | solution.py:79
  94.6 1.3 collective-permute-start.5
  96.0 1.3 collective-permute-start.6
  97.3 5.7 %collective-permute-start.7 = (bf16[128,256]{1,0:T(8,128)(2,1)S(1)}, bf16[128,256]{1,0:T(8,128)(2,1)S(1)}, u32[]{:S(2)}, u32[]{:S(2)}) collective-permute-start(bf16[128,256]{1,0:T(8,128)(2,1)S(1)} %copy-done.2), channel_id=1, source_target_pairs={{0,4},{4,8},{8,12},{12,16},{16,20},{20,24},{24,28},{1,5},{5,9},{9,... | collective-permute-start | bytes 196616 | tf_op jit(solution)/shard_map/ppermute | solution.py:14
  103.1 2.1 %collective-permute-done.7 = bf16[128,256]{1,0:T(8,128)(2,1)S(1)} collective-permute-done((bf16[128,256]{1,0:T(8,128)(2,1)S(1)}, bf16[128,256]{1,0:T(8,128)(2,1)S(1)}, u32[]{:S(2)}, u32[]{:S(2)}) %collective-permute-start.7) | collective-permute-done | bytes 65568 | tf_op jit(solution)/shard_map/ppermute | solution.py:14
  105.3 0.6 fusion.29
  105.9 0.1 fusion.8
  106.1 0.3 multiply_reduce_fusion.1
  106.4 30.0 %all-reduce.2.cloned.1.call-done = f32[3,256,256]{2,1,0:T(8,128)} async-done(((f32[3,256,256]{2,1,0:T(8,128)}), f32[3,256,256]{2,1,0:T(8,128)}) %all-reduce.2.cloned.1.call-update) | async-done | bytes 786448 | tf_op jit(solution)/shard_map/psum | solution.py:93
  136.4 1.4 fusion.5
  137.9 0.3 fusion.28
  138.2 0.2 convolution_bitcast_fusion.2
  138.4 0.4 multiply_reduce_fusion.2
  138.8 0.7 dynamic-slice_bitcast_fusion
  139.5 0.7 copy-done.4
  140.1 0.7 add_convert_fusion
  (37 shorter events, 0.3 us)
Async XLA Ops:
  7.2 98.1 %copy-start = (bf16[128,256]{1,0:T(8,128)(2,1)S(1)}, bf16[128,256]{1,0:T(8,128)(2,1)}, u32[]{:S(2)}) copy-start(bf16[128,256]{1,0:T(8,128)(2,1)} %param.9) | copy-start | bytes 196612
  7.2 129.2 %all-reduce.2.cloned.1.call-start = ((), (), s32[]{:S(2)}) async-start(), calls=%async_computation | async-start | bytes 1572864 | tf_op jit(solution)/shard_map/psum | solution.py:93
  7.2 87.4 %collective-permute-start = (bf16[128,256]{1,0:T(8,128)(2,1)}, bf16[128,256]{1,0:T(8,128)(2,1)S(1)}, u32[]{:S(2)}, u32[]{:S(2)}) collective-permute-start(bf16[128,256]{1,0:T(8,128)(2,1)} %param.10), channel_id=1, source_target_pairs={{0,16},{4,20},{8,24},{12,28},{1,17},{5,21},{9,25},{13,29},{2,18},{... | collective-permute-start | bytes 196616 | tf_op jit(solution)/shard_map/ppermute | solution.py:14
  13.2 82.8 %collective-permute-start.1 = (bf16[128,256]{1,0:T(8,128)(2,1)}, bf16[128,256]{1,0:T(8,128)(2,1)S(1)}, u32[]{:S(2)}, u32[]{:S(2)}) collective-permute-start(bf16[128,256]{1,0:T(8,128)(2,1)} %param.10), channel_id=1, source_target_pairs={{0,12},{4,16},{8,20},{12,24},{16,28},{1,13},{5,17},{9,21},{13,25},... | collective-permute-start | bytes 196616 | tf_op jit(solution)/shard_map/ppermute | solution.py:14
  17.6 79.7 %collective-permute-start.2 = (bf16[128,256]{1,0:T(8,128)(2,1)}, bf16[128,256]{1,0:T(8,128)(2,1)S(1)}, u32[]{:S(2)}, u32[]{:S(2)}) collective-permute-start(bf16[128,256]{1,0:T(8,128)(2,1)} %param.10), channel_id=1, source_target_pairs={{0,8},{4,12},{8,16},{12,20},{16,24},{20,28},{1,9},{5,13},{9,17},{1... | collective-permute-start | bytes 196616 | tf_op jit(solution)/shard_map/ppermute | solution.py:14
  18.9 84.1 %collective-permute-start.3 = (bf16[128,256]{1,0:T(8,128)(2,1)}, bf16[128,256]{1,0:T(8,128)(2,1)S(1)}, u32[]{:S(2)}, u32[]{:S(2)}) collective-permute-start(bf16[128,256]{1,0:T(8,128)(2,1)} %param.10), channel_id=1, source_target_pairs={{0,4},{4,8},{8,12},{12,16},{16,20},{20,24},{24,28},{1,5},{5,9},{9,... | collective-permute-start | bytes 196616 | tf_op jit(solution)/shard_map/ppermute | solution.py:14
  22.0 81.0 %collective-permute-start.4 = (bf16[128,256]{1,0:T(8,128)(2,1)}, bf16[128,256]{1,0:T(8,128)(2,1)S(1)}, u32[]{:S(2)}, u32[]{:S(2)}) collective-permute-start(bf16[128,256]{1,0:T(8,128)(2,1)} %param.11), channel_id=1, source_target_pairs={{0,16},{4,20},{8,24},{12,28},{1,17},{5,21},{9,25},{13,29},{2,18},{... | collective-permute-start | bytes 196616 | tf_op jit(solution)/shard_map/ppermute | solution.py:14
  55.7 0.7 copy-start.6
  55.7 0.9 copy-start.1
  56.6 0.8 copy-start.2
  59.7 0.9 copy-start.3
  94.6 8.5 %collective-permute-start.5 = (bf16[128,256]{1,0:T(8,128)(2,1)S(1)}, bf16[128,256]{1,0:T(8,128)(2,1)S(1)}, u32[]{:S(2)}, u32[]{:S(2)}) collective-permute-start(bf16[128,256]{1,0:T(8,128)(2,1)S(1)} %copy-done.2), channel_id=1, source_target_pairs={{0,12},{4,16},{8,20},{12,24},{16,28},{1,13},{5,17},{9,21},{13,25},... | collective-permute-start | bytes 196616 | tf_op jit(solution)/shard_map/ppermute | solution.py:14
  96.0 7.2 %collective-permute-start.6 = (bf16[128,256]{1,0:T(8,128)(2,1)S(1)}, bf16[128,256]{1,0:T(8,128)(2,1)S(1)}, u32[]{:S(2)}, u32[]{:S(2)}) collective-permute-start(bf16[128,256]{1,0:T(8,128)(2,1)S(1)} %copy-done.2), channel_id=1, source_target_pairs={{0,8},{4,12},{8,16},{12,20},{16,24},{20,28},{1,9},{5,13},{9,17},{1... | collective-permute-start | bytes 196616 | tf_op jit(solution)/shard_map/ppermute | solution.py:14
  97.3 8.0 %collective-permute-start.7 = (bf16[128,256]{1,0:T(8,128)(2,1)S(1)}, bf16[128,256]{1,0:T(8,128)(2,1)S(1)}, u32[]{:S(2)}, u32[]{:S(2)}) collective-permute-start(bf16[128,256]{1,0:T(8,128)(2,1)S(1)} %copy-done.2), channel_id=1, source_target_pairs={{0,4},{4,8},{8,12},{12,16},{16,20},{20,24},{24,28},{1,5},{5,9},{9,... | collective-permute-start | bytes 196616 | tf_op jit(solution)/shard_map/ppermute | solution.py:14
  138.7 0.7 copy-start.5
  139.5 0.7 copy-start.4
Sparse Core Ops, SparseCore 0:
  59.8 76.5 all-reduce.1
where the time goes:
time: 148 us
  blocking collectives  65.8 us (44%)
  waiting for transfers between devices  32.2 us (22%)
  starting transfers between devices  24.4 us (16%)
  between operations  15 us (10%)
  local copies, waits for them, and re-layouts  4.94 us (3%)
  other arithmetic  2.73 us (2%)
  matrix products  2.65 us (2%)
    all_gather x1, blocking collectives, per_device(): lax.all_gather(momentum[0], 'seq', axis=1, tiled=True)  33.4 us
    all_gather x1, blocking collectives, per_device(): lax.all_gather(owned, 'seq', axis=1, tiled=True)  32.4 us
    psum x1, waiting for transfers between devices, per_device(): lax.psum(jnp.concatenate([contract_rows(key_vectors, paired), contract_ro...  30 us
    ppermute x8, starting transfers between devices, passed_along(): lax.ppermute(value, axis, [(source, source + steps) for source in range(l...  24.4 us
    unnamed x22, local copies, waits for them, and re-layouts  3.06 us
  transfers between devices with their start and end apart: 9, of which 2 were waited for; matrix products, arithmetic and copies ran while one was open for 2% of the time, Pallas kernels for 0%

commit v1 on v0

--- a/solution.py
+++ b/solution.py
@@ -1,8 +1,11 @@
+import functools
 import math
 
 import jax
 import jax.numpy as jnp
 from jax import lax
+from jax.experimental import pallas as pl
+from jax.experimental.pallas import tpu as pltpu
 from jax.sharding import PartitionSpec as P
 
 WINDOW = 512
@@ -112,6 +115,290 @@
     return (blended, weight_new[None], moment_new[None])
 
 
+MESH = pl.DeviceIdType.MESH
+
+
+def fused_kernel(
+    count,
+    q_ref,
+    k_ref,
+    v_ref,
+    r_ref,
+    w_ref,
+    m_ref,
+    decay_ref,
+    mgain_ref,
+    wgain_ref,
+    out_ref,
+    nw_ref,
+    nm_ref,
+    wg,
+    ng,
+    kv,
+    rates,
+    gpart,
+    gin,
+    send_sems,
+    recv_sems,
+):
+    lines = count // 2
+    tokens, width = q_ref.shape
+    rows = w_ref.shape[2]
+    me = lax.axis_index("seq")
+    z, y = me // 2, me % 2
+    partner = 2 * z + (1 - y)
+    inner_rate = 0.1 / math.sqrt(tokens * count)
+    used = {"send": 0}
+    pending = []
+
+    def line_peer(step):
+        return 2 * lax.rem(z + step, lines) + y
+
+    def copy_to(src, dst, recv, device):
+        index = used["send"]
+        used["send"] += 1
+        return pltpu.make_async_remote_copy(
+            src_ref=src,
+            dst_ref=dst,
+            send_sem=send_sems.at[index],
+            recv_sem=recv_sems.at[recv],
+            device_id={"seq": device},
+            device_id_type=MESH,
+        )
+
+    def start(src, dst, recv, device, when=None):
+        copy = copy_to(src, dst, recv, device)
+        pending.append((copy, when))
+        if when is None:
+            copy.start()
+        else:
+            pl.when(when)(copy.start)
+
+    def arrived(dst, recv, when=None):
+        copy = pltpu.make_async_remote_copy(
+            src_ref=dst,
+            dst_ref=dst,
+            send_sem=send_sems.at[0],
+            recv_sem=recv_sems.at[recv],
+            device_id={"seq": partner},
+            device_id_type=MESH,
+        )
+        if when is None:
+            copy.wait_recv()
+        else:
+            pl.when(when)(copy.wait_recv)
+
+    def row_block(buffer, device):
+        return buffer.at[:, pl.ds(pl.multiple_of(device * rows, rows), rows), :]
+
+    def slot(index):
+        return kv.at[:, pl.ds(pl.multiple_of(index * tokens, tokens), tokens), :]
+
+    W_LINE, W_PAIR = 0, lines
+    N_LINE, N_PAIR = 2 * lines, 3 * lines
+    G_LINE = 4 * lines
+    KV_PAIR, RATE_PAIR, NEAR, FAR, NEAR_PAIR, FAR_PAIR = range(5 * lines, 5 * lines + 6)
+
+    barrier = pltpu.get_barrier_semaphore()
+    greeted = [partner] + [line_peer(step) for step in range(1, lines)]
+    for device in greeted:
+        pl.semaphore_signal(barrier, inc=1, device_id={"seq": device}, device_id_type=MESH)
+
+    my_rows = pl.ds(pl.multiple_of(me * rows, rows), rows)
+    wg[:, my_rows, :] = w_ref[0].astype(jnp.bfloat16)
+    my_slot = pl.ds(pl.multiple_of((4 + y) * tokens, tokens), tokens)
+    kv[0, my_slot, :] = k_ref[...]
+    kv[1, my_slot, :] = v_ref[...]
+    rates[y] = jnp.broadcast_to(r_ref[...], (tokens, 128)).T[:8]
+
+    def clear(index):
+        kv[:, index * tokens : (index + 1) * tokens, :] = jnp.zeros(
+            (2, tokens, width), jnp.bfloat16
+        )
+
+    @pl.when(z < 2)
+    def _():
+        clear(0)
+        clear(1)
+
+    @pl.when(z < 1)
+    def _():
+        clear(2)
+        clear(3)
+
+    @pl.when((z >= 2) & (y == 1))
+    def _():
+        clear(0)
+
+    pl.semaphore_wait(barrier, len(greeted))
+
+    for step in range(1, lines):
+        start(row_block(wg, me), row_block(wg, me), W_LINE + step, line_peer(step))
+    start(row_block(wg, me), row_block(wg, me), W_PAIR, partner)
+    start(rates.at[y], rates.at[y], RATE_PAIR, partner)
+    start(slot(4 + y), slot(4 + y), KV_PAIR, partner)
+    start(slot(4 + y), slot(2 + y), NEAR, 2 * (z + 1) + y, z + 1 < lines)
+
+    def forwards(buffer, line, pair):
+        for step in range(1, lines):
+            origin = line_peer(lines - step)
+            arrived(row_block(buffer, origin), line + step)
+            start(row_block(buffer, origin), row_block(buffer, origin), pair + step, partner)
+
+    def forwards_done(buffer, pair):
+        for step in range(lines):
+            origin = 2 * lax.rem(z + lines - step, lines) + (1 - y)
+            arrived(row_block(buffer, origin), pair + step)
+
+    forwards(wg, W_LINE, W_PAIR)
+    arrived(rates.at[1 - y], RATE_PAIR)
+    arrived(slot(5 - y), KV_PAIR)
+    pair_keys = kv[0, 4 * tokens : 6 * tokens, :]
+    pair_values = kv[1, 4 * tokens : 6 * tokens, :]
+    rate_cols = []
+    for index in range(2):
+        column = jnp.broadcast_to(rates[index][0:1], (128, tokens)).T
+        rate_cols.append(jnp.concatenate([column] * (width // 128), axis=1))
+    rate_all = jnp.concatenate(rate_cols, axis=0)
+    target_grad = (-(inner_rate * rate_all) * pair_values.astype(jnp.float32)).astype(
+        jnp.bfloat16
+    )
+    forwards_done(wg, W_PAIR)
+    gate_pre = jnp.dot(pair_keys, wg[0], preferred_element_type=jnp.float32)
+    up_pre = jnp.dot(pair_keys, wg[1], preferred_element_type=jnp.float32)
+    hidden_grad = lax.dot_general(
+        target_grad, wg[2], (((1,), (1,)), ((), ())), preferred_element_type=jnp.float32
+    )
+    sigmoid_x = jax.nn.sigmoid(gate_pre)
+    gate_act = gate_pre * sigmoid_x
+    hidden = (gate_act * up_pre).astype(jnp.bfloat16)
+    slope = sigmoid_x * (1.0 + gate_pre * (1.0 - sigmoid_x))
+    gate_grad = (hidden_grad * up_pre * slope).astype(jnp.bfloat16)
+    up_grad = (hidden_grad * gate_act).astype(jnp.bfloat16)
+    gpart[0] = contract_rows(pair_keys, gate_grad).astype(jnp.bfloat16)
+    gpart[1] = contract_rows(pair_keys, up_grad).astype(jnp.bfloat16)
+    gpart[2] = contract_rows(hidden, target_grad).astype(jnp.bfloat16)
+    for step in range(1, lines):
+        device = line_peer(step)
+        start(row_block(gpart, device), gin.at[step], G_LINE + step, device)
+
+    near = z >= 1
+    far = z >= 2
+    arrived(slot(2 + y), NEAR, near)
+    start(slot(2 + y), slot(y), FAR, 2 * (z + 1) + y, near & (z + 1 < lines))
+    start(slot(2 + y), slot(2 + y), NEAR_PAIR, partner, near)
+
+    old = w_ref[0]
+    total = gpart[:, my_rows, :].astype(jnp.float32)
+    for step in range(1, lines):
+        arrived(gin.at[step], G_LINE + step)
+        total += gin[step].astype(jnp.float32)
+    moment = decay_ref[0] * m_ref[0] + total
+    nm_ref[0] = moment
+    fresh = keep_scale(old - moment, old)
+    nw_ref[0] = fresh
+    ng[:, my_rows, :] = fresh.astype(jnp.bfloat16)
+    for step in range(1, lines):
+        start(row_block(ng, me), row_block(ng, me), N_LINE + step, line_peer(step))
+    start(row_block(ng, me), row_block(ng, me), N_PAIR, partner)
+
+    arrived(slot(y), FAR, far)
+    start(slot(1), slot(1), FAR_PAIR, partner, far & (y == 1))
+    forwards(ng, N_LINE, N_PAIR)
+    arrived(slot(3 - y), NEAR_PAIR, near)
+    arrived(slot(1), FAR_PAIR, far & (y == 0))
+
+    scores = lax.dot_general(
+        q_ref[...], kv[0], (((1,), (1,)), ((), ())), preferred_element_type=jnp.float32
+    ) * width ** (-0.5)
+    shape = scores.shape
+    key_index = lax.broadcasted_iota(jnp.int32, shape, 1)
+    distance = (y + 4) * tokens + lax.broadcasted_iota(jnp.int32, shape, 0) - key_index
+    key_pos = (2 * z - 4) * tokens + key_index
+    allowed = (key_pos >= 0) & (distance >= 0) & (distance < WINDOW)
+    scores = jnp.where(allowed, scores, jnp.float32(-1e30))
+    weights = jnp.exp(scores - jnp.max(scores, axis=1, keepdims=True))
+    probabilities = (weights / jnp.sum(weights, axis=1, keepdims=True)).astype(jnp.bfloat16)
+    attended = jnp.dot(probabilities, kv[1], preferred_element_type=jnp.float32)
+    attended = rms_scale(attended, wgain_ref[...])
+
+    forwards_done(ng, N_PAIR)
+    queries = q_ref[...]
+    gate_out = jnp.dot(queries, ng[0], preferred_element_type=jnp.float32)
+    up_out = jnp.dot(queries, ng[1], preferred_element_type=jnp.float32)
+    inner_act = (jax.nn.silu(gate_out) * up_out).astype(jnp.bfloat16)
+    recalled = jnp.dot(inner_act, ng[2], preferred_element_type=jnp.float32)
+    out_ref[...] = (rms_scale(recalled, mgain_ref[...]) + attended).astype(jnp.bfloat16)
+
+    for copy, when in pending:
+        if when is None:
+            copy.wait_send()
+        else:
+            pl.when(when)(copy.wait_send)
+
+
+def fused(
+    queries,
+    key_vectors,
+    values,
+    step_rates,
+    fast_weights,
+    momentum,
+    momentum_decay,
+    memory_gain,
+    window_gain,
+):
+    tokens, width = queries.shape
+    count = lax.axis_size("seq")
+    lines = count // 2
+    vmem = pl.BlockSpec(memory_space=pltpu.VMEM)
+    smem = pl.BlockSpec(memory_space=pltpu.SMEM)
+    bf16 = jnp.bfloat16
+    return pl.pallas_call(
+        functools.partial(fused_kernel, count),
+        out_shape=(
+            jax.ShapeDtypeStruct(queries.shape, bf16),
+            jax.ShapeDtypeStruct(fast_weights.shape, jnp.float32),
+            jax.ShapeDtypeStruct(momentum.shape, jnp.float32),
+        ),
+        in_specs=[vmem] * 6 + [smem] + [vmem] * 2,
+        out_specs=(vmem,) * 3,
+        scratch_shapes=[
+            pltpu.VMEM((3, width, width), bf16),
+            pltpu.VMEM((3, width, width), bf16),
+            pltpu.VMEM((2, 6 * tokens, width), bf16),
+            pltpu.VMEM((2, 8, tokens), jnp.float32),
+            pltpu.VMEM((3, width, width), bf16),
+            pltpu.VMEM((lines,) + fast_weights.shape[1:], bf16),
+            pltpu.SemaphoreType.DMA((5 * lines + 8,)),
+            pltpu.SemaphoreType.DMA((5 * lines + 6,)),
+        ],
+        compiler_params=pltpu.CompilerParams(
+            collective_id=0, has_side_effects=True, vmem_limit_bytes=32 * 1024 * 1024
+        ),
+    )(
+        queries,
+        key_vectors,
+        values,
+        step_rates,
+        fast_weights,
+        momentum,
+        momentum_decay,
+        memory_gain.reshape(1, width),
+        window_gain.reshape(1, width),
+    )
+
+
+def layer(*args):
+    tokens, width = args[0].shape
+    count = lax.axis_size("seq")
+    rows = args[4].shape[2]
+    pairs = count % 2 == 0 and count >= 4
+    if pairs and tokens == 128 and WINDOW == 4 * tokens and rows % 16 == 0 and width % 128 == 0:
+        return fused(*args)
+    return per_device(*args)
+
+
 def solution(mesh):
     in_specs = (
         P("seq", "head"),
@@ -126,5 +413,5 @@
     )
     out_specs = (P("seq", "head"), P("head", None, "seq", None), P("head", None, "seq", None))
     return jax.shard_map(
-        per_device, mesh=mesh, in_specs=in_specs, out_specs=out_specs, check_vma=False
-    )
+        layer, mesh=mesh, in_specs=in_specs, out_specs=out_specs, check_vma=False
+    )

time: 148 us -> 39.2 us (0.26)
  blocking collectives: 65.8 us -> 0 us
  waiting for transfers between devices: 32.2 us -> 0 us
  Pallas kernels: 0 us -> 31.4 us
  starting transfers between devices: 24.4 us -> 0 us
  between operations: 15 us -> 1.37 us
  other arithmetic: 2.73 us -> 0 us
  matrix products: 2.65 us -> 0 us
    all_gather x2 -> x0, blocking collectives: 65.8 us -> none  [the longest x1 33.4 us: per_device(): lax.all_gather(momentum[0], 'seq', axis=1, tiled=True)]
    pallas_call x0 -> x1, Pallas kernels: none -> 31.4 us  [fused(): pl.pallas_call(functools.partial(fused_kernel, count), out_shape=(jax.Sha...]
    psum x1 -> x0, waiting for transfers between devices: 30 us -> none  [per_device(): lax.psum(jnp.concatenate([contract_rows(key_vectors, paired), contract_ro...]
    ppermute x8 -> x0, starting transfers between devices: 24.4 us -> none  [passed_along(): lax.ppermute(value, axis, [(source, source + steps) for source in range(l...]
    unnamed x22 -> x18, local copies, waits for them, and re-layouts: 3.06 us -> 6.16 us
    dot_general x9 -> x0, matrix products: 2.65 us -> none  [the longest x1 0.65 us: per_device(): lax.dot_general(queries, context_keys, (((1,), (1,)), ((), ())), preferre...]
    ppermute x8 -> x0, waiting for transfers between devices: 2.14 us -> none  [passed_along(): lax.ppermute(value, axis, [(source, source + steps) for source in range(l...]
    reduce_sum x2 -> x0, other arithmetic: 1.55 us -> none  [the longest x1 1.44 us: keep_scale(): jnp.mean(previous * previous, axis=-1, keepdims=True) + 1e-06]
  transfers between devices with their start and end apart: 9 -> 0, of which waited for: 2 -> 0; matrix products, arithmetic and copies ran while one was open for 2% -> 0% of each run, Pallas kernels for 0% -> 0%
where the time goes in v1:
time: 39.2 us; the launch traced here: 38.9 us
  Pallas kernels  31.4 us (80%)
  local copies, waits for them, and re-layouts  6.16 us (16%)
  between operations  1.37 us (3%)
    pallas_call x1, Pallas kernels, fused(): pl.pallas_call(functools.partial(fused_kernel, count), out_shape=(jax.Sha...  31.4 us
    unnamed x18, local copies, waits for them, and re-layouts  6.16 us

profile of v1, /device:TPU:0, one launch (start us, length us, event | category | flops | bytes accessed | tf_op | source)
XLA Modules:
  0.0 38.9 jit_solution(14530503693756665143)
XLA Ops:
  0.6 0.0 copy-start.2
  1.3 0.0 copy-start.5
  1.3 0.0 copy-start.6
  1.3 0.8 %copy.12.r_ref = f32[128,1]{1,0:T(8,128)S(1)} copy(f32[128,1]{0,1:T(1,128)} %param.12) | data formatting | bytes 1024 | tf_op args[3]
  2.1 0.0 copy-done.2
  2.1 0.0 copy-done.5
  2.1 0.0 copy-done.6
  2.1 0.0 copy-start
  2.1 0.9 %copy-done = f32[1,3,32,256]{3,2,1,0:T(8,128)S(1)} copy-done((f32[1,3,32,256]{3,2,1,0:T(8,128)S(1)}, f32[1,3,32,256]{3,2,1,0:T(8,128)}, u32[]{:S(2)}) %copy-start) | copy-done | bytes 98328
  3.0 0.0 copy-start.1
  3.0 0.9 %copy-done.1 = f32[1,3,32,256]{3,2,1,0:T(8,128)S(1)} copy-done((f32[1,3,32,256]{3,2,1,0:T(8,128)S(1)}, f32[1,3,32,256]{3,2,1,0:T(8,128)}, u32[]{:S(2)}) %copy-start.1) | copy-done | bytes 98328
  3.9 0.0 copy-start.3
  3.9 0.8 %copy-done.3 = bf16[128,256]{1,0:T(8,128)(2,1)S(1)} copy-done((bf16[128,256]{1,0:T(8,128)(2,1)S(1)}, bf16[128,256]{1,0:T(8,128)(2,1)}, u32[]{:S(2)}) %copy-start.3) | copy-done | bytes 65560
  4.8 0.0 copy-start.4
  4.8 0.8 %copy-done.4 = bf16[128,256]{1,0:T(8,128)(2,1)S(1)} copy-done((bf16[128,256]{1,0:T(8,128)(2,1)S(1)}, bf16[128,256]{1,0:T(8,128)(2,1)}, u32[]{:S(2)}) %copy-start.4) | copy-done | bytes 65560
  5.6 31.4 %shard_map.112 = (bf16[128,256]{1,0:T(8,128)(2,1)S(1)}, f32[1,3,32,256]{3,2,1,0:T(8,128)S(1)}, f32[1,3,32,256]{3,2,1,0:T(8,128)S(1)}) custom-call(bf16[128,256]{1,0:T(8,128)(2,1)S(1)} %copy-done.2, bf16[128,256]{1,0:T(8,128)(2,1)S(1)} %copy-done.3, bf16[128,256]{1,0:T(8,128)(2,1)S(1)} %copy-done.4, f32[128,1]{1,0:T(8,128)S(1)} %copy.12.r_ref, ...), custom_call_target="tpu_custom_call" | custom-call | tf_op jit(solution)/shard_map/pallas_call | solution.py:357
  37.0 0.6 %copy.17 = bf16[128,256]{1,0:T(8,128)(2,1)} copy(bf16[128,256]{1,0:T(8,128)(2,1)S(1)} %get-tuple-element.6) | data formatting | bytes 131072
  37.6 0.6 %copy.18 = f32[1,3,32,256]{3,2,1,0:T(8,128)} copy(f32[1,3,32,256]{3,2,1,0:T(8,128)S(1)} %get-tuple-element.7) | data formatting | bytes 196608
  38.3 0.6 %copy.19 = f32[1,3,32,256]{3,2,1,0:T(8,128)} copy(f32[1,3,32,256]{3,2,1,0:T(8,128)S(1)} %get-tuple-element.8) | data formatting | bytes 196608
Async XLA Ops:
  0.6 1.5 %copy-start.2 = (bf16[128,256]{1,0:T(8,128)(2,1)S(1)}, bf16[128,256]{1,0:T(8,128)(2,1)}, u32[]{:S(2)}) copy-start(bf16[128,256]{1,0:T(8,128)(2,1)} %q_ref.1) | copy-start | bytes 196612
  1.3 0.8 %copy-start.5 = (f32[256]{0:T(256)S(1)}, f32[256]{0:T(256)}, u32[]{:S(2)}) copy-start(f32[256]{0:T(256)} %param.16) | copy-start | bytes 3076
  1.3 0.8 %copy-start.6 = (f32[256]{0:T(256)S(1)}, f32[256]{0:T(256)}, u32[]{:S(2)}) copy-start(f32[256]{0:T(256)} %param.17) | copy-start | bytes 3076
  2.1 0.9 %copy-start = (f32[1,3,32,256]{3,2,1,0:T(8,128)S(1)}, f32[1,3,32,256]{3,2,1,0:T(8,128)}, u32[]{:S(2)}) copy-start(f32[1,3,32,256]{3,2,1,0:T(8,128)} %w_ref.1) | copy-start | bytes 294916
  3.0 0.9 %copy-start.1 = (f32[1,3,32,256]{3,2,1,0:T(8,128)S(1)}, f32[1,3,32,256]{3,2,1,0:T(8,128)}, u32[]{:S(2)}) copy-start(f32[1,3,32,256]{3,2,1,0:T(8,128)} %m_ref.1) | copy-start | bytes 294916
  3.9 0.8 %copy-start.3 = (bf16[128,256]{1,0:T(8,128)(2,1)S(1)}, bf16[128,256]{1,0:T(8,128)(2,1)}, u32[]{:S(2)}) copy-start(bf16[128,256]{1,0:T(8,128)(2,1)} %k_ref.1) | copy-start | bytes 196612
  4.8 0.8 %copy-start.4 = (bf16[128,256]{1,0:T(8,128)(2,1)S(1)}, bf16[128,256]{1,0:T(8,128)(2,1)}, u32[]{:S(2)}) copy-start(bf16[128,256]{1,0:T(8,128)(2,1)} %v_ref.1) | copy-start | bytes 196612

commit v2 on v1

--- a/solution.py
+++ b/solution.py
@@ -9,6 +9,7 @@
 from jax.sharding import PartitionSpec as P
 
 WINDOW = 512
+VMEM_BYTES = 60 * 1024 * 1024
 
 
 def passed_along(value, axis, steps):
@@ -120,18 +121,28 @@
 
 def fused_kernel(
     count,
+    q_hbm,
+    k_hbm,
+    v_hbm,
+    r_hbm,
+    w_hbm,
+    m_hbm,
+    decay_hbm,
+    mgain_hbm,
+    wgain_hbm,
+    out_hbm,
+    nw_hbm,
+    nm_hbm,
+    out_ref,
+    nw_ref,
+    nm_ref,
     q_ref,
-    k_ref,
-    v_ref,
-    r_ref,
     w_ref,
     m_ref,
     decay_ref,
     mgain_ref,
     wgain_ref,
-    out_ref,
-    nw_ref,
-    nm_ref,
+    local_sems,
     wg,
     ng,
     kv,
@@ -205,11 +216,25 @@
         pl.semaphore_signal(barrier, inc=1, device_id={"seq": device}, device_id_type=MESH)
 
     my_rows = pl.ds(pl.multiple_of(me * rows, rows), rows)
-    wg[:, my_rows, :] = w_ref[0].astype(jnp.bfloat16)
     my_slot = pl.ds(pl.multiple_of((4 + y) * tokens, tokens), tokens)
-    kv[0, my_slot, :] = k_ref[...]
-    kv[1, my_slot, :] = v_ref[...]
-    rates[y] = jnp.broadcast_to(r_ref[...], (tokens, 128)).T[:8]
+    loads = [
+        pltpu.make_async_copy(src, dst, local_sems.at[index])
+        for index, (src, dst) in enumerate(
+            (
+                (w_hbm, w_ref),
+                (r_hbm, rates.at[y]),
+                (k_hbm, kv.at[0, my_slot, :]),
+                (v_hbm, kv.at[1, my_slot, :]),
+                (m_hbm, m_ref),
+                (q_hbm, q_ref),
+                (mgain_hbm, mgain_ref),
+                (wgain_hbm, wgain_ref),
+                (decay_hbm, decay_ref),
+            )
+        )
+    ]
+    for load in loads:
+        load.start()
 
     def clear(index):
         kv[:, index * tokens : (index + 1) * tokens, :] = jnp.zeros(
@@ -230,11 +255,15 @@
     def _():
         clear(0)
 
+    loads[0].wait()
+    wg[:, my_rows, :] = w_ref[0].astype(jnp.bfloat16)
     pl.semaphore_wait(barrier, len(greeted))
 
     for step in range(1, lines):
         start(row_block(wg, me), row_block(wg, me), W_LINE + step, line_peer(step))
     start(row_block(wg, me), row_block(wg, me), W_PAIR, partner)
+    for load in loads[1:4]:
+        load.wait()
     start(rates.at[y], rates.at[y], RATE_PAIR, partner)
     start(slot(4 + y), slot(4 + y), KV_PAIR, partner)
     start(slot(4 + y), slot(2 + y), NEAR, 2 * (z + 1) + y, z + 1 < lines)
@@ -257,7 +286,7 @@
     pair_values = kv[1, 4 * tokens : 6 * tokens, :]
     rate_cols = []
     for index in range(2):
-        column = jnp.broadcast_to(rates[index][0:1], (128, tokens)).T
+        column = jnp.broadcast_to(rates[index], (128, tokens)).T
         rate_cols.append(jnp.concatenate([column] * (width // 128), axis=1))
     rate_all = jnp.concatenate(rate_cols, axis=0)
     target_grad = (-(inner_rate * rate_all) * pair_values.astype(jnp.float32)).astype(
@@ -288,6 +317,8 @@
     start(slot(2 + y), slot(y), FAR, 2 * (z + 1) + y, near & (z + 1 < lines))
     start(slot(2 + y), slot(2 + y), NEAR_PAIR, partner, near)
 
+    for load in loads[4:]:
+        load.wait()
     old = w_ref[0]
     total = gpart[:, my_rows, :].astype(jnp.float32)
     for step in range(1, lines):
@@ -295,12 +326,16 @@
         total += gin[step].astype(jnp.float32)
     moment = decay_ref[0] * m_ref[0] + total
     nm_ref[0] = moment
+    moment_copy = pltpu.make_async_copy(nm_ref, nm_hbm, local_sems.at[9])
+    moment_copy.start()
     fresh = keep_scale(old - moment, old)
     nw_ref[0] = fresh
     ng[:, my_rows, :] = fresh.astype(jnp.bfloat16)
     for step in range(1, lines):
         start(row_block(ng, me), row_block(ng, me), N_LINE + step, line_peer(step))
     start(row_block(ng, me), row_block(ng, me), N_PAIR, partner)
+    weight_copy = pltpu.make_async_copy(nw_ref, nw_hbm, local_sems.at[10])
+    weight_copy.start()
 
     arrived(slot(y), FAR, far)
     start(slot(1), slot(1), FAR_PAIR, partner, far & (y == 1))
@@ -329,12 +364,17 @@
     inner_act = (jax.nn.silu(gate_out) * up_out).astype(jnp.bfloat16)
     recalled = jnp.dot(inner_act, ng[2], preferred_element_type=jnp.float32)
     out_ref[...] = (rms_scale(recalled, mgain_ref[...]) + attended).astype(jnp.bfloat16)
+    out_copy = pltpu.make_async_copy(out_ref, out_hbm, local_sems.at[11])
+    out_copy.start()
 
     for copy, when in pending:
         if when is None:
             copy.wait_send()
         else:
             pl.when(when)(copy.wait_send)
+    moment_copy.wait()
+    weight_copy.wait()
+    out_copy.wait()
 
 
 def fused(
@@ -351,42 +391,83 @@
     tokens, width = queries.shape
     count = lax.axis_size("seq")
     lines = count // 2
-    vmem = pl.BlockSpec(memory_space=pltpu.VMEM)
-    smem = pl.BlockSpec(memory_space=pltpu.SMEM)
+    hbm = pl.BlockSpec(memory_space=pltpu.HBM)
     bf16 = jnp.bfloat16
-    return pl.pallas_call(
+    results = pl.pallas_call(
         functools.partial(fused_kernel, count),
         out_shape=(
             jax.ShapeDtypeStruct(queries.shape, bf16),
             jax.ShapeDtypeStruct(fast_weights.shape, jnp.float32),
             jax.ShapeDtypeStruct(momentum.shape, jnp.float32),
         ),
-        in_specs=[vmem] * 6 + [smem] + [vmem] * 2,
-        out_specs=(vmem,) * 3,
+        in_specs=[hbm] * 9,
+        out_specs=(hbm,) * 3,
         scratch_shapes=[
+            pltpu.VMEM(queries.shape, bf16),
+            pltpu.VMEM(fast_weights.shape, jnp.float32),
+            pltpu.VMEM(momentum.shape, jnp.float32),
+            pltpu.VMEM(queries.shape, bf16),
+            pltpu.VMEM(fast_weights.shape, jnp.float32),
+            pltpu.VMEM(momentum.shape, jnp.float32),
+            pltpu.SMEM((1,), jnp.float32),
+            pltpu.VMEM((1, width), jnp.float32),
+            pltpu.VMEM((1, width), jnp.float32),
+            pltpu.SemaphoreType.DMA((12,)),
             pltpu.VMEM((3, width, width), bf16),
             pltpu.VMEM((3, width, width), bf16),
             pltpu.VMEM((2, 6 * tokens, width), bf16),
-            pltpu.VMEM((2, 8, tokens), jnp.float32),
+            pltpu.VMEM((2, 1, tokens), jnp.float32),
             pltpu.VMEM((3, width, width), bf16),
             pltpu.VMEM((lines,) + fast_weights.shape[1:], bf16),
             pltpu.SemaphoreType.DMA((5 * lines + 8,)),
             pltpu.SemaphoreType.DMA((5 * lines + 6,)),
         ],
         compiler_params=pltpu.CompilerParams(
-            collective_id=0, has_side_effects=True, vmem_limit_bytes=32 * 1024 * 1024
+            collective_id=0, has_side_effects=True, vmem_limit_bytes=VMEM_BYTES
         ),
     )(
         queries,
         key_vectors,
         values,
-        step_rates,
+        step_rates.reshape(1, tokens),
         fast_weights,
         momentum,
         momentum_decay,
         memory_gain.reshape(1, width),
         window_gain.reshape(1, width),
     )
+    return store(results)
+
+
+def store_kernel(*refs):
+    sources, targets, held, sems = refs[:3], refs[3:6], refs[6:9], refs[9]
+    loads = [
+        pltpu.make_async_copy(src, mid, sems.at[index])
+        for index, (src, mid) in enumerate(zip(sources, held))
+    ]
+    stores = [
+        pltpu.make_async_copy(mid, dst, sems.at[3 + index])
+        for index, (mid, dst) in enumerate(zip(held, targets))
+    ]
+    for load in loads:
+        load.start()
+    for load, copy in zip(loads, stores):
+        load.wait()
+        copy.start()
+    for copy in stores:
+        copy.wait()
+
+
+def store(results):
+    return pl.pallas_call(
+        store_kernel,
+        out_shape=tuple(jax.ShapeDtypeStruct(x.shape, x.dtype) for x in results),
+        in_specs=[pl.BlockSpec(memory_space=pltpu.HBM)] * 3,
+        out_specs=(pl.BlockSpec(memory_space=pltpu.HBM),) * 3,
+        scratch_shapes=[pltpu.VMEM(x.shape, x.dtype) for x in results]
+        + [pltpu.SemaphoreType.DMA((6,))],
+        compiler_params=pltpu.CompilerParams(vmem_limit_bytes=VMEM_BYTES),
+    )(*results)
 
 
 def layer(*args):

time: 39.2 us -> 35.1 us (0.90)
  local copies, waits for them, and re-layouts: 6.16 us -> 0 us
  Pallas kernels: 31.4 us -> 33.6 us
    unnamed x18 -> x0, local copies, waits for them, and re-layouts: 6.16 us -> none
    pallas_call x0 -> x1, Pallas kernels: none -> 1.67 us  [store(): pl.pallas_call(store_kernel, out_shape=tuple((jax.ShapeDtypeStruct(x.shap...]
    pallas_call x1, Pallas kernels: 31.4 us -> 32 us  [fused(): pl.pallas_call(functools.partial(fused_kernel, count), out_shape=(jax.Sha...]
where the time goes in v2:
time: 35.1 us; the launch traced here: 34.9 us
  Pallas kernels  33.6 us (96%)
  between operations  1.29 us (4%)
    pallas_call x1, Pallas kernels, fused(): pl.pallas_call(functools.partial(fused_kernel, count), out_shape=(jax.Sha...  32 us
    pallas_call x1, Pallas kernels, store(): pl.pallas_call(store_kernel, out_shape=tuple((jax.ShapeDtypeStruct(x.shap...  1.67 us

profile of v2, /device:TPU:0, one launch (start us, length us, event | category | flops | bytes accessed | tf_op | source)
XLA Modules:
  0.0 34.9 jit_solution(7852775446702501029)
XLA Ops:
  1.3 32.0 %shard_map.112 = (bf16[128,256]{1,0:T(8,128)(2,1)}, f32[1,3,32,256]{3,2,1,0:T(8,128)}, f32[1,3,32,256]{3,2,1,0:T(8,128)}) custom-call(bf16[128,256]{1,0:T(8,128)(2,1)} %q_hbm.1, bf16[128,256]{1,0:T(8,128)(2,1)} %k_hbm.1, bf16[128,256]{1,0:T(8,128)(2,1)} %v_hbm.1, f32[1,128]{1,0:T(1,128)} %bitcast.5, f32[1,3,32,256]{3,2,1,0:T(8,128)} %w_hbm.1, ...), custom_call_target="tpu_custom_call" | custom-call | tf_op jit(solution)/shard_map/pallas_call | solution.py:396
  33.2 1.7 %shard_map.113 = (bf16[128,256]{1,0:T(8,128)(2,1)}, f32[1,3,32,256]{3,2,1,0:T(8,128)}, f32[1,3,32,256]{3,2,1,0:T(8,128)}) custom-call(bf16[128,256]{1,0:T(8,128)(2,1)} %get-tuple-element.6.refs_0_, f32[1,3,32,256]{3,2,1,0:T(8,128)} %get-tuple-element.7.refs_1_, f32[1,3,32,256]{3,2,1,0:T(8,128)} %get-tuple-element.8.refs_2_), custom_call_target="tpu_custom_call" | custom-call | tf_op jit(solution)/shard_map/pallas_call | solution.py:462
